TPU v7x, 32 devices: a whole 2x2x4 slice. The times are simulated.
32 devices in a mesh: dp: 16 (over z, y, core), mlp: 2 (over x).
Axes of the slice: x: 2, y: 2, z: 4, core: 2. Of those that a mesh axis runs over, the one named last changes fastest.
Arguments:
- block_input: bfloat16 [32768, 512], P(('dp', 'mlp')), may hold values from -6 to 6
- doc_lengths: int32 [32, 4], P(('dp', 'mlp')), may hold values from 0 to 1024, as said below
- norm_gain: bfloat16 [2, 512], replicated, may hold values from 0.25 to 1.75
- norm_bias: bfloat16 [2, 512], replicated, may hold values from -1.75 to 1.75
- qkv_weight: bfloat16 [2, 512, 1536], replicated, may hold values from -0.25 to 0.25
- qkv_bias: bfloat16 [2, 1536], replicated, may hold values from -3 to 3
- out_weight: bfloat16 [2, 512, 512], replicated, may hold values from -1 to 1
- out_bias: bfloat16 [2, 512], replicated, may hold values from -1.75 to 1.75
- up_weight: bfloat16 [2, 512, 2048], P(None, None, 'mlp'), may hold values from -0.25 to 0.25
- up_bias: bfloat16 [2, 2048], P(None, 'mlp'), may hold values from -3 to 3
- down_weight: bfloat16 [2, 2048, 512], P(None, 'mlp'), may hold values from -0.125 to 0.125
- down_bias: bfloat16 [2, 512], replicated, may hold values from -1.75 to 1.75
- out_grad: bfloat16 [32768, 512], P(('dp', 'mlp')), may hold values from -6 to 6
Outputs:
- block_output: bfloat16 [32768, 512], P(('dp', 'mlp'))
- input_grad: float32 [32768, 512], P(('dp', 'mlp'))
- norm_gain_grad: float32 [2, 512], replicated
- norm_bias_grad: float32 [2, 512], replicated
- qkv_weight_grad: float32 [2, 512, 1536], replicated
- qkv_bias_grad: float32 [2, 1536], replicated
- out_weight_grad: float32 [2, 512, 512], replicated
- out_bias_grad: float32 [2, 512], replicated
- up_weight_grad: float32 [2, 512, 2048], P(None, None, 'mlp')
- up_bias_grad: float32 [2, 2048], P(None, 'mlp')
- down_weight_grad: float32 [2, 2048, 512], P(None, 'mlp')
- down_bias_grad: float32 [2, 512], replicated
Inputs may be any that keep to these rules, and one draw needn't show every extreme that they name: `doc_lengths`: each device's 4 lengths add up to 1024; a length of 0 is an empty slot; on one device a single document fills all 1024 rows.
All inputs are finite; a program needn't handle non-finite values.
Results may differ from a plain program's by a relative error of at most 0.012.
Values may be sent and summed in bfloat16 or wider, within the bound.
A program may use at most 256 MiB of HBM per device.

v0:
```python
import jax
import jax.numpy as jnp
from jax import lax
from jax.sharding import PartitionSpec as P

HEADS = 8
ROT = 16


norm_eps = 1e-05
rotary_base = 10000.0


def layer_norm(values, gain_row, bias_row):
    centre = jnp.mean(values, axis=-1, keepdims=True)
    centred = values - centre
    spread = jnp.mean(centred * centred, axis=-1, keepdims=True)
    return centred * lax.rsqrt(spread + norm_eps) * gain_row + bias_row


def doc_layout(lengths, row_count):
    ends = jnp.cumsum(lengths)
    starts = ends - lengths
    row_index = jnp.arange(row_count, dtype=jnp.int32)
    doc_owner = jnp.sum((row_index[:, None] >= ends[None, :]).astype(jnp.int32), axis=1)
    matched = doc_owner[:, None] == jnp.arange(lengths.shape[0], dtype=jnp.int32)[None, :]
    doc_start = jnp.sum(jnp.where(matched, starts[None, :], 0), axis=1)
    allowed = (doc_owner[:, None] == doc_owner[None, :]) & (
        row_index[None, :] <= row_index[:, None]
    )
    return (allowed, row_index - doc_start)


def rotary_tables(position, rot_dims):
    half_dims = rot_dims // 2
    freqs = rotary_base ** (-(2.0 * jnp.arange(half_dims, dtype=jnp.float32) / rot_dims))
    angles = position.astype(jnp.float32)[:, None] * freqs[None, :]
    return (jnp.cos(angles), jnp.sin(angles))


def rotate(heads_in, cosines, sine_table, rot_dims):
    half_dims = rot_dims // 2
    first_half = heads_in[..., :half_dims]
    second_half = heads_in[..., half_dims:rot_dims]
    remainder = heads_in[..., rot_dims:]
    cos_rows = cosines[:, None, :]
    sin_rows = sine_table[:, None, :]
    return jnp.concatenate(
        [
            first_half * cos_rows - second_half * sin_rows,
            second_half * cos_rows + first_half * sin_rows,
            remainder,
        ],
        axis=-1,
    )


def gelu_exact(values):
    return jax.nn.gelu(values, approximate=False)


def attention_inputs(packed, cosines, sine_table, head_count):
    row_count = packed.shape[0]
    model_width = packed.shape[1] // 3
    head_shape = (row_count, head_count, model_width // head_count)
    queries = rotate(packed[:, :model_width].reshape(head_shape), cosines, sine_table, ROT).astype(
        jnp.bfloat16
    )
    key_rows = rotate(
        packed[:, model_width : 2 * model_width].reshape(head_shape), cosines, sine_table, ROT
    ).astype(jnp.bfloat16)
    value_rows = packed[:, 2 * model_width :].reshape(head_shape).astype(jnp.bfloat16)
    return (queries, key_rows, value_rows)


def attend_rows(query_block, key_rows, allowed_block, score_scale):
    scores = (
        jnp.einsum("qhd,khd->hqk", query_block, key_rows, preferred_element_type=jnp.float32)
        * score_scale
    )
    scores = jnp.where(allowed_block[None, :, :], scores, -1e30)
    row_top = jnp.max(scores, axis=-1, keepdims=True)
    expo = jnp.exp(scores - row_top)
    return expo / jnp.sum(expo, axis=-1, keepdims=True)


def attention_forward(queries, key_rows, value_rows, allowed, block_rows):
    row_count, head_count, head_size = queries.shape
    score_scale = head_size ** (-0.5)
    block_count = row_count // block_rows

    def one_block(inputs_pair):
        query_block, allowed_block = inputs_pair
        weights_low = attend_rows(query_block, key_rows, allowed_block, score_scale).astype(
            jnp.bfloat16
        )
        return jnp.einsum(
            "hqk,khd->qhd", weights_low, value_rows, preferred_element_type=jnp.float32
        )

    mixed = lax.map(
        one_block,
        (
            queries.reshape(block_count, block_rows, head_count, head_size),
            allowed.reshape(block_count, block_rows, row_count),
        ),
    )
    return mixed.reshape(row_count, head_count * head_size).astype(jnp.bfloat16)


def attention_backward(queries, key_rows, value_rows, grad_mixed, allowed, block_rows):
    row_count, head_count, head_size = queries.shape
    score_scale = head_size ** (-0.5)
    block_count = row_count // block_rows

    def one_block(carry, inputs_triple):
        grad_keys, grad_values = carry
        query_block, grad_block, allowed_block = inputs_triple
        attend_weights = attend_rows(query_block, key_rows, allowed_block, score_scale)
        grad_weights = jnp.einsum(
            "qhd,khd->hqk", grad_block, value_rows, preferred_element_type=jnp.float32
        )
        row_total = jnp.sum(grad_weights * attend_weights, axis=-1, keepdims=True)
        grad_scores = (attend_weights * (grad_weights - row_total)).astype(jnp.bfloat16)
        grad_query = (
            jnp.einsum("hqk,khd->qhd", grad_scores, key_rows, preferred_element_type=jnp.float32)
            * score_scale
        )
        grad_keys = (
            grad_keys
            + jnp.einsum(
                "hqk,qhd->khd", grad_scores, query_block, preferred_element_type=jnp.float32
            )
            * score_scale
        )
        grad_values = grad_values + jnp.einsum(
            "hqk,qhd->khd",
            attend_weights.astype(jnp.bfloat16),
            grad_block,
            preferred_element_type=jnp.float32,
        )
        return ((grad_keys, grad_values), grad_query)

    start_zero = jnp.zeros(queries.shape, jnp.float32)
    scanned = (
        queries.reshape(block_count, block_rows, head_count, head_size),
        grad_mixed.reshape(block_count, block_rows, head_count, head_size),
        allowed.reshape(block_count, block_rows, row_count),
    )
    (grad_keys, grad_values), grad_query = lax.scan(one_block, (start_zero, start_zero), scanned)
    return (grad_query.reshape(queries.shape), grad_keys, grad_values)


def mlp_forward(hidden, params):
    up_part, up_shift, down_part = params
    pre_act = jnp.dot(
        lax.all_gather(hidden, "mlp", axis=0, tiled=True),
        up_part,
        preferred_element_type=jnp.float32,
    ) + up_shift.astype(jnp.float32)
    partial_out = jnp.dot(
        gelu_exact(pre_act).astype(jnp.bfloat16), down_part, preferred_element_type=jnp.float32
    )
    return lax.psum_scatter(partial_out, "mlp", scatter_dimension=0, tiled=True)


def body(
    block_input,
    doc_lengths,
    norm_gain,
    norm_bias,
    qkv_weight,
    qkv_bias,
    out_weight,
    out_bias,
    up_weight,
    up_bias,
    down_weight,
    down_bias,
    out_grad,
):
    row_count, model_width = block_input.shape
    layers = norm_gain.shape[0]
    head_count = HEADS
    head_size = model_width // head_count
    block_rows = min(row_count, 512)
    allowed, position = doc_layout(doc_lengths[0], row_count)
    cosines, sine_table = rotary_tables(position, ROT)
    stream = block_input.astype(jnp.float32)
    kept_inputs = []
    kept_params = []
    for layer_index in range(layers):
        kept_inputs.append(stream)
        params = (up_weight[layer_index], up_bias[layer_index], down_weight[layer_index])
        kept_params.append(params)
        hidden = layer_norm(
            stream,
            norm_gain[layer_index].astype(jnp.float32),
            norm_bias[layer_index].astype(jnp.float32),
        ).astype(jnp.bfloat16)
        packed = jnp.dot(
            hidden, qkv_weight[layer_index], preferred_element_type=jnp.float32
        ) + qkv_bias[layer_index].astype(jnp.float32)
        queries, key_rows, value_rows = attention_inputs(packed, cosines, sine_table, head_count)
        mixed = attention_forward(queries, key_rows, value_rows, allowed, block_rows)
        attn_out = jnp.dot(
            mixed, out_weight[layer_index], preferred_element_type=jnp.float32
        ) + out_bias[layer_index].astype(jnp.float32)
        stream = (
            stream
            + attn_out
            + mlp_forward(hidden, params)
            + down_bias[layer_index].astype(jnp.float32)
        )
    block_output = stream.astype(jnp.bfloat16)
    grad_stream = out_grad.astype(jnp.float32)
    grads_by_layer = [None] * layers
    for layer_index in reversed(range(layers)):
        stream = kept_inputs[layer_index]
        up_part, up_shift, down_part = kept_params[layer_index]
        grad_low = grad_stream.astype(jnp.bfloat16)
        normed, norm_pull = jax.vjp(
            layer_norm,
            stream,
            norm_gain[layer_index].astype(jnp.float32),
            norm_bias[layer_index].astype(jnp.float32),
        )
        hidden = normed.astype(jnp.bfloat16)
        packed = jnp.dot(
            hidden, qkv_weight[layer_index], preferred_element_type=jnp.float32
        ) + qkv_bias[layer_index].astype(jnp.float32)
        queries, key_rows, value_rows = attention_inputs(packed, cosines, sine_table, head_count)
        mixed = attention_forward(queries, key_rows, value_rows, allowed, block_rows)
        grad_out_w = jnp.einsum("td,te->de", mixed, grad_low, preferred_element_type=jnp.float32)
        grad_out_b = jnp.sum(grad_low.astype(jnp.float32), axis=0)
        grad_mixed = jnp.einsum(
            "te,de->td", grad_low, out_weight[layer_index], preferred_element_type=jnp.float32
        ).astype(jnp.bfloat16)
        grad_query, grad_keys, grad_values = attention_backward(
            queries,
            key_rows,
            value_rows,
            grad_mixed.reshape(row_count, head_count, head_size),
            allowed,
            block_rows,
        )
        grad_query = rotate(grad_query, cosines, -sine_table, ROT)
        grad_keys = rotate(grad_keys, cosines, -sine_table, ROT)
        grad_packed = jnp.concatenate(
            [
                grad_query.reshape(row_count, model_width),
                grad_keys.reshape(row_count, model_width),
                grad_values.reshape(row_count, model_width),
            ],
            axis=1,
        ).astype(jnp.bfloat16)
        grad_qkv_w = jnp.einsum(
            "td,te->de", hidden, grad_packed, preferred_element_type=jnp.float32
        )
        grad_qkv_b = jnp.sum(grad_packed.astype(jnp.float32), axis=0)
        grad_hidden = jnp.einsum(
            "te,de->td", grad_packed, qkv_weight[layer_index], preferred_element_type=jnp.float32
        )
        hidden_all, grad_all = (
            lax.all_gather(hidden, "mlp", axis=0, tiled=True),
            lax.all_gather(grad_low, "mlp", axis=0, tiled=True),
        )
        pre_act = jnp.dot(
            hidden_all, up_part, preferred_element_type=jnp.float32
        ) + up_shift.astype(jnp.float32)
        activ, gelu_pull = jax.vjp(gelu_exact, pre_act)
        grad_down_w = jnp.einsum(
            "tf,td->fd", activ.astype(jnp.bfloat16), grad_all, preferred_element_type=jnp.float32
        )
        grad_activ = jnp.einsum(
            "td,fd->tf", grad_all, down_part, preferred_element_type=jnp.float32
        )
        grad_pre = gelu_pull(grad_activ)[0].astype(jnp.bfloat16)
        grad_up_w = jnp.einsum(
            "td,tf->df", hidden_all, grad_pre, preferred_element_type=jnp.float32
        )
        grad_up_b = jnp.sum(grad_pre.astype(jnp.float32), axis=0)
        grad_back_rows = jnp.einsum(
            "tf,df->td", grad_pre, up_part, preferred_element_type=jnp.float32
        )
        grad_hidden = grad_hidden + lax.psum_scatter(
            grad_back_rows, "mlp", scatter_dimension=0, tiled=True
        )
        grad_input, grad_gain, grad_bias = norm_pull(grad_hidden)
        grad_stream = grad_stream + grad_input
        grad_up_w, grad_up_b, grad_down_w = lax.psum((grad_up_w, grad_up_b, grad_down_w), "dp")
        grad_gain, grad_bias, grad_qkv_w, grad_qkv_b, grad_out_w, grad_out_b = lax.psum(
            (grad_gain, grad_bias, grad_qkv_w, grad_qkv_b, grad_out_w, grad_out_b), ("dp", "mlp")
        )
        grads_by_layer[layer_index] = (
            grad_gain,
            grad_bias,
            grad_qkv_w,
            grad_qkv_b,
            grad_out_w,
            grad_out_b,
            grad_up_w,
            grad_up_b,
            grad_down_w,
        )
    stacked = [
        jnp.stack([grads_by_layer[layer_index][member_index] for layer_index in range(layers)])
        for member_index in range(9)
    ]
    (
        gain_all,
        bias_all,
        qkv_w_all,
        qkv_b_all,
        out_w_all,
        out_b_all,
        up_w_all,
        up_b_all,
        down_w_all,
    ) = stacked
    return (
        block_output,
        grad_stream,
        gain_all,
        bias_all,
        qkv_w_all,
        qkv_b_all,
        out_w_all,
        out_b_all,
        up_w_all,
        up_b_all,
        down_w_all,
        out_b_all,
    )


def solution(mesh):
    placed = (
        P(("dp", "mlp"), None),
        P(("dp", "mlp"), None),
        P(),
        P(),
        P(),
        P(),
        P(),
        P(),
        P(None, None, "mlp"),
        P(None, "mlp"),
        P(None, "mlp", None),
        P(),
        P(("dp", "mlp"), None),
    )
    return jax.shard_map(
        body,
        mesh=mesh,
        in_specs=placed,
        out_specs=(
            P(("dp", "mlp"), None),
            P(("dp", "mlp"), None),
            P(),
            P(),
            P(),
            P(),
            P(),
            P(),
            P(None, None, "mlp"),
            P(None, "mlp"),
            P(None, "mlp", None),
            P(),
        ),
        check_vma=False,
    )
```

profile of v0, /device:TPU:0, one launch (start us, length us, event | category | flops | bytes accessed | tf_op | source)
XLA Modules:
  0.0 1256.5 jit_solution(3819806072926654004)
XLA Ops:
  37.1 11.3 all-gather.5.cloned.1.call-done
  48.4 23.5 %multiply_convert_fusion.3 = (bf16[2048,1024]{1,0:T(8,128)(2,1)S(1)}, f32[2048,1024]{1,0:T(8,128)}, f32[2048,1024]{1,0:T(8,128)}) fusion(f32[1024]{0:T(1024)S(1)} %bitcast.366, bf16[2048,512]{0,1:T(8,128)(2,1)} %all-gather.5.cloned.1.call-done, bf16[2,512,1024]{2,1,0:T(8,128)(2,1)} %param.29), kind=kOutput, calls=%fused_computation.123 | convolution fusion | flops 2285895680 | bytes 24121344 | tf_op jit(solution)/shard_map/dot_general | solution.py:156
  79.6 82.3 %while.58 = (s32[]{:T(128)}, bf16[2,512,8,64]{1,3,2,0:T(8,128)(2,1)}, pred[2,512,1024]{2,1,0:T(8,128)(4,1)S(1)}, bf16[2,512,8,64]{1,3,2,0:T(8,128)(2,1)S(1)}, bf...) while((s32[]{:T(128)}, bf16[2,512,8,64]{1,3,2,0:T(8,128)(2,1)}, ...), condition=%wide.region_8.9_spmd, body=%wide.region_5.8_spmd.sunk | while | flops 1107297280 | bytes 72385104 | solution.py:101
  89.6 22.1 %fusion.252 = (f32[8,512]{1,0:T(8,128)S(1)}, f32[8,512,1024]{2,1,0:T(8,128)}) fusion(f32[8,512,1024]{2,1,0:T(8,128)} %fusion.251, pred[512,1024]{1,0:T(8,128)(4,1)} %dynamic-slice_bitcast_fusion.8), kind=kOutput, calls=%fused_computation.306.clone.1 | output fusion | flops 25166848 | bytes 34095104 | tf_op jit(solution)/shard_map/while/body/eval_jaxpr/sub | solution.py:83
  130.3 22.1 %fusion.252 = (f32[8,512]{1,0:T(8,128)S(1)}, f32[8,512,1024]{2,1,0:T(8,128)}) fusion(f32[8,512,1024]{2,1,0:T(8,128)} %fusion.251, pred[512,1024]{1,0:T(8,128)(4,1)} %dynamic-slice_bitcast_fusion.8), kind=kOutput, calls=%fused_computation.306.clone.1 | output fusion | flops 25166848 | bytes 34095104 | tf_op jit(solution)/shard_map/while/body/eval_jaxpr/sub | solution.py:83
  216.3 23.7 %multiply_convert_fusion.2 = (bf16[2048,1024]{1,0:T(8,128)(2,1)}, f32[2048,1024]{1,0:T(8,128)}, f32[2048,1024]{1,0:T(8,128)}) fusion(f32[1024]{0:T(1024)S(1)} %bitcast.368, bf16[2048,512]{0,1:T(8,128)(2,1)} %all-gather.7.cloned.1.call-done, bf16[2,512,1024]{2,1,0:T(8,128)(2,1)} %param.29), kind=kOutput, calls=%fused_computation.110 | convolution fusion | flops 2285895680 | bytes 24121344 | tf_op jit(solution)/shard_map/dot_general | solution.py:156
  241.6 11.7 convert_reduce_fusion
  261.9 188.8 %while.60 = (s32[]{:T(128)}, f32[1024,8,64]{0,2,1:T(8,128)S(1)}, f32[1024,8,64]{0,2,1:T(8,128)}, f32[2,512,8,64]{1,0,3,2:T(2,128)}, bf16[2,512,8,64]{1,3,2,0:T(8...) while((s32[]{:T(128)}, f32[1024,8,64]{0,2,1:T(8,128)S(1)}, ...), condition=%wide.region_21.22_spmd.clone, body=%wide.region_17.21_spmd.clone.sunk | while | flops 2750149632 | bytes 226068208 | solution.py:150
  272.4 22.0 %fusion.270 = (f32[8,512]{1,0:T(8,128)S(1)}, f32[8,512,1024]{2,1,0:T(8,128)}) fusion(f32[8,512,1024]{2,1,0:T(8,128)} %fusion.269, pred[512,1024]{1,0:T(8,128)(4,1)} %dynamic-slice_bitcast_fusion.10), kind=kOutput, calls=%fused_computation.308.clone.1 | output fusion | flops 25166848 | bytes 34095104 | tf_op jit(solution)/shard_map/while/body/eval_jaxpr/sub | solution.py:83
  303.6 10.7 multiply_reduce_fusion.7
  314.3 11.5 multiply_convert_fusion.6
  331.2 19.6 %dynamic_update_slice.25 = f32[2,512,8,64]{1,0,3,2:T(2,128)} dynamic-update-slice(f32[2,512,8,64]{1,0,3,2:T(2,128)} %get-tuple-element.818, f32[1,512,8,64]{1,0,3,2:T(1,128)} %copy.160, s32[]{:T(128)} %get-tuple-element.815, s32[]{:T(128)} %constant.48.clone.1..sunk, s32[]{:T(128)} %constant.48.clone.1..sunk, s32[]{:T(128)} %constant.48.clone.1..sunk) | dynamic-update-slice | bytes 2097156 | tf_op jit(solution)/shard_map/while/body/jit(dynamic_update_index_in_dim)/dynamic_update_slice | solution.py:101
  366.3 22.0 %fusion.270 = (f32[8,512]{1,0:T(8,128)S(1)}, f32[8,512,1024]{2,1,0:T(8,128)}) fusion(f32[8,512,1024]{2,1,0:T(8,128)} %fusion.269, pred[512,1024]{1,0:T(8,128)(4,1)} %dynamic-slice_bitcast_fusion.10), kind=kOutput, calls=%fused_computation.308.clone.1 | output fusion | flops 25166848 | bytes 34095104 | tf_op jit(solution)/shard_map/while/body/eval_jaxpr/sub | solution.py:83
  398.0 10.6 multiply_reduce_fusion.7
  408.6 11.5 multiply_convert_fusion.6
  425.5 19.6 %dynamic_update_slice.25 = f32[2,512,8,64]{1,0,3,2:T(2,128)} dynamic-update-slice(f32[2,512,8,64]{1,0,3,2:T(2,128)} %get-tuple-element.818, f32[1,512,8,64]{1,0,3,2:T(1,128)} %copy.160, s32[]{:T(128)} %get-tuple-element.815, s32[]{:T(128)} %constant.48.clone.1..sunk, s32[]{:T(128)} %constant.48.clone.1..sunk, s32[]{:T(128)} %constant.48.clone.1..sunk) | dynamic-update-slice | bytes 2097156 | tf_op jit(solution)/shard_map/while/body/jit(dynamic_update_index_in_dim)/dynamic_update_slice | solution.py:101
  471.5 82.2 %while.59 = (s32[]{:T(128)}, bf16[2,512,8,64]{1,3,2,0:T(8,128)(2,1)}, pred[2,512,1024]{2,1,0:T(8,128)(4,1)S(1)}, bf16[2,512,8,64]{1,3,2,0:T(8,128)(2,1)S(1)}, bf...) while((s32[]{:T(128)}, bf16[2,512,8,64]{1,3,2,0:T(8,128)(2,1)}, ...), condition=%wide.region_15.16_spmd, body=%wide.region_12.15_spmd.sunk | while | flops 1107297280 | bytes 72385104 | solution.py:101
  481.3 22.0 %fusion.258 = (f32[8,512]{1,0:T(8,128)S(1)}, f32[8,512,1024]{2,1,0:T(8,128)}) fusion(f32[8,512,1024]{2,1,0:T(8,128)} %fusion.257, pred[512,1024]{1,0:T(8,128)(4,1)} %dynamic-slice_bitcast_fusion.9), kind=kOutput, calls=%fused_computation.307.clone.1 | output fusion | flops 25166848 | bytes 34095104 | tf_op jit(solution)/shard_map/while/body/eval_jaxpr/sub | solution.py:83
  521.8 22.0 %fusion.258 = (f32[8,512]{1,0:T(8,128)S(1)}, f32[8,512,1024]{2,1,0:T(8,128)}) fusion(f32[8,512,1024]{2,1,0:T(8,128)} %fusion.257, pred[512,1024]{1,0:T(8,128)(4,1)} %dynamic-slice_bitcast_fusion.9), kind=kOutput, calls=%fused_computation.307.clone.1 | output fusion | flops 25166848 | bytes 34095104 | tf_op jit(solution)/shard_map/while/body/eval_jaxpr/sub | solution.py:83
  579.8 189.1 %while.61 = (s32[]{:T(128)}, f32[1024,8,64]{0,2,1:T(8,128)S(1)}, f32[1024,8,64]{0,2,1:T(8,128)}, f32[2,512,8,64]{1,0,3,2:T(2,128)}, bf16[2,512,8,64]{1,3,2,0:T(8...) while((s32[]{:T(128)}, f32[1024,8,64]{0,2,1:T(8,128)S(1)}, ...), condition=%wide.region_29.30_spmd.clone, body=%wide.region_25.29_spmd.clone.sunk | while | flops 2750149632 | bytes 226068208 | solution.py:150
  590.2 22.2 %fusion.282 = (f32[8,512]{1,0:T(8,128)S(1)}, f32[8,512,1024]{2,1,0:T(8,128)}) fusion(f32[8,512,1024]{2,1,0:T(8,128)} %fusion.281, pred[512,1024]{1,0:T(8,128)(4,1)} %dynamic-slice_bitcast_fusion.11), kind=kOutput, calls=%fused_computation.309.clone.1 | output fusion | flops 25166848 | bytes 34095104 | tf_op jit(solution)/shard_map/while/body/eval_jaxpr/sub | solution.py:83
  621.6 10.6 multiply_reduce_fusion.8
  632.2 11.5 multiply_convert_fusion.7
  649.1 19.6 %dynamic_update_slice.26 = f32[2,512,8,64]{1,0,3,2:T(2,128)} dynamic-update-slice(f32[2,512,8,64]{1,0,3,2:T(2,128)} %get-tuple-element.851, f32[1,512,8,64]{1,0,3,2:T(1,128)} %copy.161, s32[]{:T(128)} %get-tuple-element.848, s32[]{:T(128)} %constant.48.clone.1..sunk.1, s32[]{:T(128)} %constant.48.clone.1..sunk.1, s32[]{:T(128)} %constant.48.clone.1..sunk.1) | dynamic-update-slice | bytes 2097156 | tf_op jit(solution)/shard_map/while/body/jit(dynamic_update_index_in_dim)/dynamic_update_slice | solution.py:101
  684.3 22.2 %fusion.282 = (f32[8,512]{1,0:T(8,128)S(1)}, f32[8,512,1024]{2,1,0:T(8,128)}) fusion(f32[8,512,1024]{2,1,0:T(8,128)} %fusion.281, pred[512,1024]{1,0:T(8,128)(4,1)} %dynamic-slice_bitcast_fusion.11), kind=kOutput, calls=%fused_computation.309.clone.1 | output fusion | flops 25166848 | bytes 34095104 | tf_op jit(solution)/shard_map/while/body/eval_jaxpr/sub | solution.py:83
  726.8 11.5 multiply_convert_fusion.7
  743.7 19.6 %dynamic_update_slice.26 = f32[2,512,8,64]{1,0,3,2:T(2,128)} dynamic-update-slice(f32[2,512,8,64]{1,0,3,2:T(2,128)} %get-tuple-element.851, f32[1,512,8,64]{1,0,3,2:T(1,128)} %copy.161, s32[]{:T(128)} %get-tuple-element.848, s32[]{:T(128)} %constant.48.clone.1..sunk.1, s32[]{:T(128)} %constant.48.clone.1..sunk.1, s32[]{:T(128)} %constant.48.clone.1..sunk.1) | dynamic-update-slice | bytes 2097156 | tf_op jit(solution)/shard_map/while/body/jit(dynamic_update_index_in_dim)/dynamic_update_slice | solution.py:101
  833.3 34.7 %all-reduce.2 = (f32[1,1024]{1,0:T(1,128)S(1)}, f32[1,1024]{1,0:T(1,128)S(1)}) all-reduce(f32[1,1024]{1,0:T(1,128)S(1)} %bitcast.364, f32[1,1024]{1,0:T(1,128)S(1)} %bitcast.365), channel_id=1, replica_groups=mesh['dp'=16,'mlp'=2] {'dp'}, use_global_device_ids=true, to_apply=%region_58.59 | all-reduce | flops 2048 | bytes 16384 | tf_op jit(solution)/shard_map/psum | solution.py:291
  868.6 94.5 %all-reduce.7.cloned.1.call-done = (f32[1,512,1536]{2,1,0:T(8,128)}, f32[1,512,1536]{2,1,0:T(8,128)}, f32[1,512,512]{2,1,0:T(8,128)}, f32[1,512,512]{2,1,0:T(8,128)}) async-done(((f32[1,512,1536]{2,1,0:T(8,128)}, f32[1,512,1536]{2,1,0:T(8,128)}, f32[1,512,512]{2,1,0:T(8,128)}, f32[1,512,512]{2,1,0:T(8,128)}), (f32[1,512,1536]{2,1,0:T(8,128)}, f32[1,512,1536]{2,1,0:T(8,128)}, f32[1,512,512]{2,1,0:T(8,128)}, ...) | async-done | bytes 8388624 | tf_op jit(solution)/shard_map/psum | solution.py:292
  971.3 168.1 %all-reduce.9.cloned.1.call-done = (f32[1,512,1024]{2,1,0:T(8,128)}, f32[1,512,1024]{2,1,0:T(8,128)}, f32[1,1024,512]{2,1,0:T(8,128)}, f32[1,1024,512]{2,1,0:T(8,128)}) async-done(((f32[1,512,1024]{2,1,0:T(8,128)}, f32[1,512,1024]{2,1,0:T(8,128)}, f32[1,1024,512]{2,1,0:T(8,128)}, f32[1,1024,512]{2,1,0:T(8,128)}), (f32[1,512,1024]{2,1,0:T(8,128)}, f32[1,512,1024]{2,1,0:T(8,128)}, f32[1,1024,512]{2,1,0:T(8,128)}, ...) | async-done | bytes 8388624 | tf_op jit(solution)/shard_map/psum | solution.py:291
  1146.7 49.1 %reduce-scatter.11.cloned.1.call-done = f32[1024,512]{0,1:T(8,128)} async-done(((f32[2048,512]{0,1:T(8,128)}), f32[1024,512]{0,1:T(8,128)}) %reduce-scatter.11.cloned.1.call-update) | async-done | bytes 2097168 | tf_op jit(solution)/shard_map/reduce_scatter | solution.py:286
  1204.4 39.7 %all-reduce = (f32[1,512]{1,0:T(1,128)S(1)}, f32[1,512]{1,0:T(1,128)S(1)}, f32[1,512]{1,0:T(1,128)S(1)}, f32[1,512]{1,0:T(1,128)S(1)}, f32[1,1536]{1,0:T(1,128)S...) all-reduce(f32[1,512]{1,0:T(1,128)S(1)} %bitcast.370, ...), channel_id=1, replica_groups=mesh['dp'=16,'mlp'=2] {'dp','mlp'}, use_global_device_ids=true, to_apply=%region_36.37 | all-reduce | flops 6144 | bytes 49152 | tf_op jit(solution)/shard_map/psum | solution.py:292
  (426 shorter events, 449.7 us)
Async XLA Ops:
  7.2 41.2 %all-gather.5.cloned.1.call-start = ((), (), s32[]{:S(2)}) async-start(), calls=%async_computation.4 | async-start | bytes 3145728 | tf_op jit(solution)/shard_map/all_gather | solution.py:157
  12.5 155.1 %reduce-scatter.5.cloned.1.call-start = ((), (), s32[]{:S(2)}) async-start(), calls=%async_computation.5 | async-start | bytes 6291456 | tf_op jit(solution)/shard_map/reduce_scatter | solution.py:164
  35.9 36.0 %copy-start.89 = (f32[1,1024]{1,0:T(1,128)}, f32[1,1024]{1,0:T(1,128)S(1)}, u32[]{:S(2)}) copy-start(f32[1,1024]{1,0:T(1,128)S(1)} %get-tuple-element.533) | copy-start | bytes 12292
  48.4 25.6 %copy-start.96 = (bf16[2,1024,512]{2,1,0:T(8,128)(2,1)S(1)}, bf16[2,1024,512]{2,1,0:T(8,128)(2,1)}, u32[]{:S(2)}) copy-start(bf16[2,1024,512]{2,1,0:T(8,128)(2,1)} %param.31) | copy-start | bytes 6291460
  78.5 137.7 %all-gather.7.cloned.1.call-start = ((), (), s32[]{:S(2)}) async-start(), calls=%async_computation.6 | async-start | bytes 3145728 | tf_op jit(solution)/shard_map/all_gather | solution.py:157
  173.7 67.9 %all-gather.9.cloned.1.call-start = ((), (), s32[]{:S(2)}) async-start(), calls=%async_computation.8 | async-start | bytes 3145728 | tf_op jit(solution)/shard_map/all_gather | solution.py:266
  174.3 285.8 %reduce-scatter.9.cloned.1.call-start = ((), (), s32[]{:S(2)}) async-start(), calls=%async_computation.9 | async-start | bytes 6291456 | tf_op jit(solution)/shard_map/reduce_scatter | solution.py:286
  241.6 13.8 %copy-start.99 = (bf16[2,512,1024]{2,1,0:T(8,128)(2,1)S(1)}, bf16[2,512,1024]{2,1,0:T(8,128)(2,1)}, u32[]{:S(2)}) copy-start(bf16[2,512,1024]{2,1,0:T(8,128)(2,1)} %param.29) | copy-start | bytes 6291460
  259.8 533.1 %all-gather.11.cloned.1.call-start = ((), (), s32[]{:S(2)}) async-start(), calls=%async_computation.10 | async-start | bytes 3145728 | tf_op jit(solution)/shard_map/all_gather | solution.py:266
  262.3 9.3 copy-start.6
  356.2 9.3 copy-start.6
  388.3 9.7 copy-start.46
  388.3 9.7 copy-start.51
  470.4 358.6 %reduce-scatter.7.cloned.1.call-start = ((), (), s32[]{:S(2)}) async-start(), calls=%async_computation.7 | async-start | bytes 6291456 | tf_op jit(solution)/shard_map/reduce_scatter | solution.py:164
  567.2 395.9 %all-reduce.7.cloned.1.call-start = ((), (), s32[]{:S(2)}) async-start(), calls=%async_computation.12 | async-start | bytes 16777216 | tf_op jit(solution)/shard_map/psum | solution.py:292
  570.5 9.3 copy-start.3
  570.5 9.3 copy-start.4
  580.0 9.3 copy-start.8
  674.2 9.3 copy-start.8
  706.5 9.7 copy-start.47
  706.5 9.7 copy-start.48
  782.4 357.0 %all-reduce.9.cloned.1.call-start = ((), (), s32[]{:S(2)}) async-start(), calls=%async_computation.13 | async-start | bytes 16777216 | tf_op jit(solution)/shard_map/psum | solution.py:291
  799.7 11.9 copy-start.101
  815.3 380.4 %reduce-scatter.11.cloned.1.call-start = ((), (), s32[]{:S(2)}) async-start(), calls=%async_computation.11 | async-start | bytes 6291456 | tf_op jit(solution)/shard_map/reduce_scatter | solution.py:286
  1144.3 51.4 %copy-start.12 = (bf16[1024,512]{0,1:T(8,128)(2,1)S(1)}, bf16[1024,512]{0,1:T(8,128)(2,1)}, u32[]{:S(2)}) copy-start(bf16[1024,512]{0,1:T(8,128)(2,1)} %copy-done.11) | copy-start | bytes 3145732
  1144.3 51.4 %copy-start.25 = (bf16[1024,8,64]{0,2,1:T(8,128)(2,1)S(1)}, bf16[1024,8,64]{0,2,1:T(8,128)(2,1)}, u32[]{:S(2)}) copy-start(bf16[1024,8,64]{0,2,1:T(8,128)(2,1)} %copy-done.24) | copy-start | bytes 3145732
  1144.3 51.4 %copy-start.61 = (f32[1024]{0:T(1024)S(1)}, f32[1024]{0:T(1024)}, u32[]{:S(2)}) copy-start(f32[1024]{0:T(1024)} %copy-done.60) | copy-start | bytes 12292
  1144.3 51.4 %copy-start.75 = (f32[1,512]{1,0:T(1,128)S(1)}, f32[1,512]{1,0:T(1,128)}, u32[]{:S(2)}) copy-start(f32[1,512]{1,0:T(1,128)} %copy-done.74) | copy-start | bytes 6148
  1146.6 53.9 %copy-start.69 = (f32[1024]{0:T(1024)S(1)}, f32[1024]{0:T(1024)}, u32[]{:S(2)}) copy-start(f32[1024]{0:T(1024)} %copy-done.68) | copy-start | bytes 12292
  1146.7 53.9 %copy-start.63 = (f32[1024]{0:T(1024)S(1)}, f32[1024]{0:T(1024)}, u32[]{:S(2)}) copy-start(f32[1024]{0:T(1024)} %copy-done.62) | copy-start | bytes 12292
  1146.7 54.8 %copy-start.19 = (bf16[1024,512]{0,1:T(8,128)(2,1)S(1)}, bf16[1024,512]{0,1:T(8,128)(2,1)}, u32[]{:S(2)}) copy-start(bf16[1024,512]{0,1:T(8,128)(2,1)} %copy.108) | copy-start | bytes 3145732
  1146.7 54.8 %copy-start.67 = (f32[1024]{0:T(1024)S(1)}, f32[1024]{0:T(1024)}, u32[]{:S(2)}) copy-start(f32[1024]{0:T(1024)} %copy-done.66) | copy-start | bytes 12292
  (95 other events, 382.4 us)
Sparse Core Ops, SparseCore 0:
  12.6 35.8 all-gather.4
  78.6 54.3 reduce-scatter.4
  173.9 33.1 all-gather.6
  208.5 33.1 all-gather.8
  259.9 54.3 reduce-scatter.8
  470.5 33.6 all-gather.10
  567.3 54.6 reduce-scatter.6
  782.5 180.4 all-reduce.6
  968.4 171.0 all-reduce.8
  1141.6 54.1 reduce-scatter.10
where the time goes:
time: 1270 us; the launch traced here: 1260 us
  matrix products  369 us (29%)
  waiting for transfers between devices  325 us (26%)
  other arithmetic  274 us (22%)
  local copies, waits for them, and re-layouts  196 us (15%)
  blocking collectives  74.4 us (6%)
  between operations  15.4 us (1%)
    sub x8, other arithmetic, attend_rows(): expo = jnp.exp(scores - row_top)  177 us
    psum x1, waiting for transfers between devices, body(): lax.psum((grad_up_w, grad_up_b, grad_down_w), 'dp')  168 us
    psum x1, waiting for transfers between devices, body(): lax.psum((grad_gain, grad_bias, grad_qkv_w, grad_qkv_b, grad_out_w, grad_...  94.5 us
    dynamic_update_slice x8, local copies, waits for them, and re-layouts, attention_forward(): lax.map(one_block, (queries.reshape(block_count, block_rows, head_count,...  86.8 us
    dot_general x8, matrix products, attend_rows(): jnp.einsum('qhd,khd->hqk', query_block, key_rows, preferred_element_type=...  71.1 us
    reduce_scatter x2, waiting for transfers between devices, body(): lax.psum_scatter(grad_back_rows, 'mlp', scatter_dimension=0, tiled=True)  49.1 us
    dot_general x2, matrix products, mlp_forward(): jnp.dot(lax.all_gather(hidden, 'mlp', axis=0, tiled=True), up_part, prefe...  47.2 us
    convert_element_type x4, other arithmetic, one_block(): (attend_weights * (grad_weights - row_total)).astype(jnp.bfloat16)  46.1 us
  transfers between devices with their start and end apart: 10, of which 5 were waited for; matrix products, arithmetic and copies ran while one was open for 59% of the time, Pallas kernels for 0%

commit v1 on v0

v1 whole, which is shorter than its diff:
```python
import functools
import math

import jax
import jax.numpy as jnp
from jax import lax
from jax.experimental import pallas as pl
from jax.experimental.pallas import tpu as pltpu
from jax.sharding import PartitionSpec as P

HEADS = 8
ROT = 16
HALF = ROT // 2
BLK = 256
norm_eps = 1e-05
rotary_base = 10000.0
bf16 = jnp.bfloat16
f32 = jnp.float32
NEG = -1e30
LOG2E = math.log2(math.e)
LN2 = math.log(2.0)


def dot_nn(a, b):
    return lax.dot_general(a, b, (((1,), (0,)), ((), ())), preferred_element_type=f32)


def dot_nt(a, b):
    return lax.dot_general(a, b, (((1,), (1,)), ((), ())), preferred_element_type=f32)


def dot_tn(a, b):
    return lax.dot_general(a, b, (((0,), (0,)), ((), ())), preferred_element_type=f32)


def row_of(ref, layer):
    return ref[...].astype(f32)[layer : layer + 1, :]


def doc_tables(lens, rows):
    lane = lax.broadcasted_iota(jnp.int32, (HALF, rows), 1)
    sub = lax.broadcasted_iota(jnp.int32, (HALF, rows), 0)
    start = jnp.int32(0)
    hot = jnp.zeros((HALF, rows), f32)
    first = jnp.zeros((HALF, rows), jnp.int32)
    for slot in range(lens.shape[1]):
        end = start + lens[0, slot]
        inside = (lane >= start) & (lane < end)
        hot = jnp.where(inside & (sub == slot), 1.0, hot)
        first = jnp.where(inside, start, first)
        start = end
    return hot, lane - first


def rotary_tables(position):
    index = lax.broadcasted_iota(jnp.int32, position.shape, 0).astype(f32)
    freqs = jnp.exp(index * (-2.0 / ROT * math.log(rotary_base)))
    angles = position.astype(f32) * freqs
    return jnp.cos(angles), jnp.sin(angles)


def rotate(values, cosines, sines):
    size = 64
    heads = values.shape[0] // size
    split = values.reshape(heads, size, values.shape[1])
    first, second, rest = split[:, :HALF], split[:, HALF:ROT], split[:, ROT:]
    turned = jnp.concatenate(
        [first * cosines - second * sines, second * cosines + first * sines, rest], axis=1
    )
    return turned.reshape(values.shape)


def mask_rows(hot):
    sub = lax.broadcasted_iota(jnp.int32, hot.shape, 0)
    rows = jnp.where(sub < 4, jnp.where(hot > 0.0, 0.0, NEG), jnp.where(sub < 7, 1.0, 0.0))
    return rows


def causal_bias():
    row = lax.broadcasted_iota(jnp.int32, (BLK, BLK), 0)
    col = lax.broadcasted_iota(jnp.int32, (BLK, BLK), 1)
    return jnp.where(row <= col, 0.0, NEG)


def norm_stats(values):
    centre = jnp.mean(values, axis=-1, keepdims=True)
    centred = values - centre
    spread = jnp.mean(centred * centred, axis=-1, keepdims=True)
    return centred, lax.rsqrt(spread + norm_eps)


def split3(value):
    a = value.astype(bf16).astype(f32)
    rest = value - a
    b = rest.astype(bf16).astype(f32)
    return jnp.concatenate([a, b, rest - b], axis=0)


def attention_forward(qkv, mix, lse, hot_s, mask_s, tri, krow, scores, probs, group):
    tokens = qkv.shape[1]
    width = qkv.shape[0] // 3
    blocks = tokens // BLK

    def heads(step, carry):
        tops = [{} for _ in range(group)]
        sums = [{} for _ in range(group)]
        rows = [pl.multiple_of((step * group + j) * 64, 64) for j in range(group)]
        for j in range(group):
            keyed = jnp.concatenate(
                [
                    qkv[pl.ds(width + rows[j], 64), :],
                    mask_s[...],
                    jnp.zeros((48, tokens), bf16),
                ],
                axis=0,
            )
            krow[j] = keyed.T
        for stage in range(group + 2):
            for i in range(blocks):
                n = (i + 1) * BLK
                at = slice(i * BLK, n)
                if stage < group:
                    j = stage
                    query = jnp.concatenate(
                        [qkv[pl.ds(rows[j], 64), at], hot_s[:, at], jnp.zeros((48, BLK), bf16)],
                        axis=0,
                    )
                    raw = dot_nn(krow[j, 0:n, :], query)
                    diagonal = raw[i * BLK :] + tri[...]
                    top = jnp.max(diagonal, axis=0, keepdims=True)
                    if i:
                        top = jnp.maximum(top, jnp.max(raw[: i * BLK], axis=0, keepdims=True))
                        scores[j % 2, i, 0 : i * BLK, :] = raw[: i * BLK]
                    scores[j % 2, i, i * BLK : n, :] = diagonal
                    tops[j][i] = top
                if 0 <= stage - 1 < group:
                    j = stage - 1
                    weights = jnp.exp2(scores[j % 2, i, 0:n, :] - tops[j][i])
                    sums[j][i] = jnp.sum(weights, axis=0, keepdims=True)
                    probs[j % 2, i, 0:n, :] = weights.astype(bf16)
                if 0 <= stage - 2 < group:
                    j = stage - 2
                    out = dot_nn(qkv[pl.ds(2 * width + rows[j], 64), 0:n], probs[j % 2, i, 0:n, :])
                    mix[pl.ds(rows[j], 64), at] = (out / sums[j][i]).astype(bf16)
                    lse[pl.ds(step * group + j, 1), at] = tops[j][i] + jnp.log2(sums[j][i])
        return carry

    lax.fori_loop(0, HEADS // group, heads, 0)


def forward_kernel(
    lens,
    block_input,
    gain,
    bias,
    qkv_bias,
    out_bias,
    up_bias,
    down_bias,
    qkv_w_h,
    out_w_h,
    up_w_h,
    down_w_h,
    block_output,
    stream_h,
    hid_h,
    qkv_h,
    mix_h,
    lse_h,
    act_h,
    slope_h,
    stream,
    hidden,
    hid,
    qkv,
    mix,
    lse,
    act,
    slope,
    qkv_w,
    out_w,
    up_w,
    down_w,
    qkv_b,
    pre,
    hot_s,
    mask_s,
    cos_s,
    sin_s,
    tri,
    krow,
    scores,
    probs,
    in_sem,
    out_sem,
):
    tokens, width = block_input.shape
    layers = gain.shape[0]
    hidden_units = up_w.shape[2]
    blocks = tokens // BLK
    loads = [
        [
            pltpu.make_async_copy(src.at[layer], dst.at[layer], in_sem.at[layer, k])
            for k, (src, dst) in enumerate(
                ((qkv_w_h, qkv_w), (out_w_h, out_w), (up_w_h, up_w), (down_w_h, down_w))
            )
        ]
        for layer in range(layers)
    ]
    for layer in range(layers):
        for copy in loads[layer]:
            copy.start()
    hot, position = doc_tables(lens, tokens)
    zeros8 = jnp.zeros_like(hot)
    hot_s[...] = jnp.concatenate([hot, zeros8], axis=0).astype(bf16)
    mask_s[...] = jnp.concatenate([mask_rows(hot), zeros8], axis=0).astype(bf16)
    cos_s[...], sin_s[...] = rotary_tables(position)
    tri[...] = causal_bias()
    stream[...] = block_input[...].astype(f32)
    stores = []
    for layer in range(layers):
        gain_row, bias_row = row_of(gain, layer), row_of(bias, layer)
        qkv_b[...] = jnp.broadcast_to(row_of(qkv_bias, layer), (128, 3 * width)).T

        for copy in stores:
            copy.wait()
        stores = []

        def norm_block(i, carry):
            rows = pl.ds(pl.multiple_of(i * BLK, BLK), BLK)
            centred, scale = norm_stats(stream[rows, :])
            low = (centred * scale * gain_row + bias_row).astype(bf16)
            hidden[rows, :] = low
            hid[:, rows] = low.T
            return carry

        lax.fori_loop(0, blocks, norm_block, 0)
        loads[layer][0].wait()
        for part in range(3):
            cols = slice(part * width, (part + 1) * width)
            for i in range(blocks):
                at = slice(i * BLK, (i + 1) * BLK)
                value = dot_tn(qkv_w[layer, :, cols], hid[:, at])
                column = qkv_b[cols, :]
                value = value + jnp.concatenate([column] * (BLK // 128), axis=1)
                if part < 2:
                    value = rotate(value, cos_s[:, at], sin_s[:, at])
                if part == 0:
                    value = value * (64**-0.5 * LOG2E)
                qkv[cols, at] = value.astype(bf16)
        attention_forward(qkv, mix, lse, hot_s, mask_s, tri, krow, scores, probs, 4)

        def save(src, dst, k):
            copy = pltpu.make_async_copy(src, dst.at[layer], out_sem.at[k])
            copy.start()
            stores.append(copy)

        save(hid, hid_h, 0)
        save(qkv, qkv_h, 1)
        save(mix, mix_h, 2)
        save(lse, lse_h, 3)
        for k in range(1, 4):
            loads[layer][k].wait()
        shift = row_of(out_bias, layer) + row_of(down_bias, layer)
        up_row = row_of(up_bias, layer)
        chunk = 512

        def mlp_block(i, carry):
            rows = pl.ds(pl.multiple_of(i * BLK, BLK), BLK)
            for c in range(hidden_units // chunk):
                cs = slice(c * chunk, (c + 1) * chunk)
                pre[:, cs] = dot_nn(hidden[rows, :], up_w[layer, :, cs]) + up_row[:, cs]
            for c in range(hidden_units // chunk):
                cs = slice(c * chunk, (c + 1) * chunk)
                u = pre[:, cs]
                cdf = 0.5 + 0.5 * lax.erf(u * (2.0**-0.5))
                pdf = jnp.exp2(u * u * (-0.5 * LOG2E)) * ((2.0 * math.pi) ** -0.5)
                act[rows, cs] = (u * cdf).astype(bf16)
                slope[rows, cs] = (cdf + u * pdf).astype(bf16)
            total = dot_tn(mix[:, rows], out_w[layer]) + dot_nn(act[rows, :], down_w[layer])
            stream[rows, :] = stream[rows, :] + (total + shift)
            return carry

        lax.fori_loop(0, blocks, mlp_block, 0)
        save(act, act_h, 4)
        save(slope, slope_h, 5)
        if layer + 1 < layers:
            copy = pltpu.make_async_copy(stream, stream_h, out_sem.at[6])
            copy.start()
            stores.append(copy)
    block_output[...] = stream[...].astype(bf16)
    for copy in stores:
        copy.wait()


def attention_backward(qkv, mix, grad_mix, lse, hot_s, mask_s, tri, cos_s, sin_s, work, group):
    krow, vrow, qext, gext, probs, dscore = work
    tokens = qkv.shape[1]
    width = qkv.shape[0] // 3
    blocks = tokens // BLK
    ones = jnp.where(lax.broadcasted_iota(jnp.int32, (64, tokens), 0) < 3, 1.0, 0.0).astype(bf16)

    def heads(step, carry):
        rows = [pl.multiple_of((step * group + j) * 64, 64) for j in range(group)]
        for j in range(group):
            r = rows[j]
            keyed = jnp.concatenate(
                [qkv[pl.ds(width + r, 64), :], mask_s[...], jnp.zeros((48, tokens), bf16)], axis=0
            )
            krow[j] = keyed.T
            vrow[j] = jnp.concatenate([qkv[pl.ds(2 * width + r, 64), :], ones], axis=0).T
            grad = grad_mix[pl.ds(r, 64), :].astype(f32)
            total = jnp.sum(grad * mix[pl.ds(r, 64), :].astype(f32), axis=0, keepdims=True)
            qext[j] = jnp.concatenate(
                [
                    qkv[pl.ds(r, 64), :].astype(f32),
                    hot_s[0:4, :].astype(f32),
                    split3(-lse[pl.ds(step * group + j, 1), :]),
                    jnp.zeros((57, tokens), f32),
                ],
                axis=0,
            ).astype(bf16)
            gext[j] = jnp.concatenate(
                [grad, split3(-total), jnp.zeros((61, tokens), f32)], axis=0
            ).astype(bf16)
        for j in range(group):
            r = rows[j]
            for i in range(blocks):
                n = (i + 1) * BLK
                at = slice(i * BLK, n)
                raw = dot_nn(krow[j, 0:n, :], qext[j, :, at])
                if i:
                    raw = jnp.concatenate([raw[: i * BLK], raw[i * BLK :] + tri[...]], axis=0)
                else:
                    raw = raw + tri[...]
                weights = jnp.exp2(raw)
                slopes = dot_nn(vrow[j, 0:n, :], gext[j, :, at])
                dscore[j, 0:n, at] = (weights * slopes).astype(bf16)
                probs[j, 0:n, at] = weights.astype(bf16)
            dq, dk, dv = [], [], []
            for i in range(blocks):
                n = (i + 1) * BLK
                at = slice(i * BLK, n)
                dq.append(dot_nn(qkv[pl.ds(width + r, 64), 0:n], dscore[j, 0:n, at]))
                dk.append(dot_nt(qkv[pl.ds(r, 64), i * BLK :], dscore[j, at, i * BLK :]))
                dv.append(dot_nt(grad_mix[pl.ds(r, 64), i * BLK :], probs[j, at, i * BLK :]))
            dq = jnp.concatenate(dq, axis=1) * 64**-0.5
            dk = jnp.concatenate(dk, axis=1) * LN2
            qkv[pl.ds(r, 64), :] = rotate(dq, cos_s[...], -sin_s[...]).astype(bf16)
            qkv[pl.ds(width + r, 64), :] = rotate(dk, cos_s[...], -sin_s[...]).astype(bf16)
            qkv[pl.ds(2 * width + r, 64), :] = jnp.concatenate(dv, axis=1).astype(bf16)
        return carry

    lax.fori_loop(0, HEADS // group, heads, 0)


def backward_kernel(
    lens,
    block_input,
    out_grad,
    gain,
    bias,
    qkv_w_h,
    out_w_h,
    up_w_h,
    down_w_h,
    stream_h,
    hid_h,
    qkv_h,
    mix_h,
    lse_h,
    act_h,
    slope_h,
    input_grad,
    mlp_grad,
    att_grad,
    vec_grad,
    stream,
    grad_low,
    grad_mix,
    grad_hid,
    hid,
    qkv,
    mix,
    lse,
    act,
    slope,
    qkv_w,
    out_w,
    up_w,
    down_w,
    hot_s,
    mask_s,
    cos_s,
    sin_s,
    tri,
    krow,
    vrow,
    qext,
    gext,
    probs,
    dscore,
    in_sem,
):
    tokens, width = block_input.shape
    layers = gain.shape[0]
    hidden_units = up_w.shape[1]
    blocks = tokens // BLK
    grad = input_grad

    def load(src, dst, layer, k):
        copy = pltpu.make_async_copy(src, dst, in_sem.at[layer, k])
        copy.start()
        return copy

    def load_mlp(layer):
        return [
            load(slope_h.at[layer], slope, layer, 0),
            load(down_w_h.at[layer], down_w, layer, 1),
            load(act_h.at[layer], act, layer, 2),
            load(up_w_h.at[layer], up_w, layer, 3),
            load(hid_h.at[layer], hid.at[layer, 0:width, :], layer, 4),
        ]

    def load_att(layer):
        copies = [
            load(qkv_h.at[layer], qkv, layer, 5),
            load(mix_h.at[layer], mix, layer, 6),
            load(lse_h.at[layer], lse, layer, 7),
        ]
        return copies

    last = layers - 1
    mlp_loads, att_loads = load_mlp(last), load_att(last)
    weight_loads = [
        load(out_w_h, out_w, 0, 8),
        load(qkv_w_h, qkv_w, 0, 9),
        load(stream_h, stream, 0, 10),
    ]
    hot, position = doc_tables(lens, tokens)
    zeros8 = jnp.zeros_like(hot)
    hot_s[...] = jnp.concatenate([hot, zeros8], axis=0).astype(bf16)
    mask_s[...] = jnp.concatenate([mask_rows(hot), zeros8], axis=0).astype(bf16)
    cos_s[...], sin_s[...] = rotary_tables(position)
    tri[...] = causal_bias()
    for layer in range(layers):
        hid[layer, width : width + 16, :] = jnp.ones((16, tokens), bf16)
    grad[...] = out_grad[...].astype(f32)
    grad_low[...] = out_grad[...]
    for layer in reversed(range(layers)):
        mlp_loads[0].wait()
        mlp_loads[1].wait()
        mlp_loads[3].wait()

        def mlp_block(i, carry):
            rows = pl.ds(pl.multiple_of(i * BLK, BLK), BLK)
            for c in range(hidden_units // 512):
                cs = slice(c * 512, (c + 1) * 512)
                da = dot_nt(grad_low[rows, :], down_w[cs, :])
                slope[rows, cs] = (slope[rows, cs].astype(f32) * da).astype(bf16)
            grad_hid[rows, :] = dot_nt(slope[rows, :], up_w[...])
            return carry

        lax.fori_loop(0, blocks, mlp_block, 0)
        mlp_loads[2].wait()
        mlp_loads[4].wait()
        half = hidden_units // 2
        for c in range(hidden_units // 512):
            x, at = divmod(c * 512, half)
            cs = slice(c * 512, (c + 1) * 512)
            mlp_grad[layer, x, half + at : half + at + 512, :] = dot_tn(
                act[:, cs], grad_low[...]
            ).astype(bf16)
            up = dot_nn(hid[layer], slope[:, cs])
            mlp_grad[layer, x, at : at + 512, :] = up[:width].astype(bf16)
            vec_grad[layer, 6 + c : 7 + c, :] = up[width : width + 1]
        if layer:
            mlp_loads = load_mlp(layer - 1)
        if layer == last:
            weight_loads[0].wait()
            weight_loads[1].wait()
            weight_loads[2].wait()
        for copy in att_loads:
            copy.wait()
        att_grad[layer, 3 * width : 4 * width, :] = dot_nn(mix[...], grad_low[...]).astype(bf16)
        vec_grad[layer, 5:6, :] = jnp.sum(grad_low[...].astype(f32), axis=0, keepdims=True)
        grad_mix[...] = dot_nt(out_w[layer], grad_low[...]).astype(bf16)
        attention_backward(
            qkv,
            mix,
            grad_mix,
            lse,
            hot_s,
            mask_s,
            tri,
            cos_s,
            sin_s,
            (krow, vrow, qext, gext, probs, dscore),
            2,
        )
        for part in range(3):
            cols = slice(part * width, (part + 1) * width)
            got = dot_nt(hid[layer], qkv[cols, :])
            att_grad[layer, cols, :] = got[:width].astype(bf16)
            vec_grad[layer, 2 + part : 3 + part, :] = got[width : width + 1]
        gain_row = row_of(gain, layer)
        vec_grad[layer, 0:2, :] = jnp.zeros((2, width), f32)

        def norm_block(i, carry):
            rows = pl.ds(pl.multiple_of(i * BLK, BLK), BLK)
            back = lax.dot_general(
                qkv[:, rows],
                qkv_w[layer],
                (((0,), (1,)), ((), ())),
                preferred_element_type=f32,
            )
            dh = grad_hid[rows, :] + back
            if layer:
                centred, scale = norm_stats(stream[rows, :])
            else:
                centred, scale = norm_stats(block_input[rows, :].astype(f32))
            n = centred * scale
            product = dh * n
            vec_grad[layer, 0:1, :] += jnp.sum(product, axis=0, keepdims=True)
            vec_grad[layer, 1:2, :] += jnp.sum(dh, axis=0, keepdims=True)
            e = dh * gain_row
            mean_e = jnp.mean(e, axis=-1, keepdims=True)
            mean_en = jnp.mean(product * gain_row, axis=-1, keepdims=True)
            total = grad[rows, :] + scale * (e - mean_e - n * mean_en)
            grad[rows, :] = total
            if layer:
                grad_low[rows, :] = total.astype(bf16)
            return carry

        lax.fori_loop(0, blocks, norm_block, 0)
        if layer:
            att_loads = load_att(layer - 1)


VMEM = pl.BlockSpec(memory_space=pltpu.VMEM)
SMEM = pl.BlockSpec(memory_space=pltpu.SMEM)
ANY = pl.BlockSpec(memory_space=pl.ANY)


def run_forward(lens, block_input, gain, bias, qkv_b, out_b, up_b, down_b, qkv_w, out_w, up_w, down_w):
    tokens, width = block_input.shape
    layers = gain.shape[0]
    units = up_w.shape[2]
    shape = jax.ShapeDtypeStruct
    v = pltpu.VMEM
    return pl.pallas_call(
        forward_kernel,
        out_shape=(
            shape((tokens, width), bf16),
            shape((tokens, width), f32),
            shape((layers, width, tokens), bf16),
            shape((layers, 3 * width, tokens), bf16),
            shape((layers, width, tokens), bf16),
            shape((layers, HEADS, tokens), f32),
            shape((layers, tokens, units), bf16),
            shape((layers, tokens, units), bf16),
        ),
        in_specs=[SMEM] + [VMEM] * 7 + [ANY] * 4,
        out_specs=(VMEM,) + (ANY,) * 7,
        scratch_shapes=[
            v((tokens, width), f32),
            v((tokens, width), bf16),
            v((width, tokens), bf16),
            v((3 * width, tokens), bf16),
            v((width, tokens), bf16),
            v((HEADS, tokens), f32),
            v((tokens, units), bf16),
            v((tokens, units), bf16),
            v((layers, width, 3 * width), bf16),
            v((layers, width, width), bf16),
            v((layers, width, units), bf16),
            v((layers, units, width), bf16),
            v((3 * width, 128), f32),
            v((BLK, units), f32),
            v((16, tokens), bf16),
            v((16, tokens), bf16),
            v((HALF, tokens), f32),
            v((HALF, tokens), f32),
            v((BLK, BLK), f32),
            v((4, tokens, 128), bf16),
            v((2, tokens // BLK, tokens, BLK), f32),
            v((2, tokens // BLK, tokens, BLK), bf16),
            pltpu.SemaphoreType.DMA((layers, 4)),
            pltpu.SemaphoreType.DMA((7,)),
        ],
        compiler_params=pltpu.CompilerParams(vmem_limit_bytes=63 * 2**20),
        name="forward",
    )(lens, block_input, gain, bias, qkv_b, out_b, up_b, down_b, qkv_w, out_w, up_w, down_w)


def run_backward(lens, block_input, out_grad, gain, bias, qkv_w, out_w, up_w, down_w, saved):
    tokens, width = block_input.shape
    layers = gain.shape[0]
    units = up_w.shape[2]
    shape = jax.ShapeDtypeStruct
    v = pltpu.VMEM
    return pl.pallas_call(
        backward_kernel,
        out_shape=(
            shape((tokens, width), f32),
            shape((layers, 2, units, width), bf16),
            shape((layers, 4 * width, width), bf16),
            shape((layers, 16, width), f32),
        ),
        in_specs=[SMEM] + [VMEM] * 4 + [ANY] * 11,
        out_specs=(VMEM,) * 4,
        scratch_shapes=[
            v((tokens, width), f32),
            v((tokens, width), bf16),
            v((width, tokens), bf16),
            v((tokens, width), f32),
            v((layers, width + 16, tokens), bf16),
            v((3 * width, tokens), bf16),
            v((width, tokens), bf16),
            v((HEADS, tokens), f32),
            v((tokens, units), bf16),
            v((tokens, units), bf16),
            v((layers, width, 3 * width), bf16),
            v((layers, width, width), bf16),
            v((width, units), bf16),
            v((units, width), bf16),
            v((16, tokens), bf16),
            v((16, tokens), bf16),
            v((HALF, tokens), f32),
            v((HALF, tokens), f32),
            v((BLK, BLK), f32),
            v((2, tokens, 128), bf16),
            v((2, tokens, 128), bf16),
            v((2, 128, tokens), bf16),
            v((2, 128, tokens), bf16),
            v((2, tokens, tokens), bf16),
            v((2, tokens, tokens), bf16),
            pltpu.SemaphoreType.DMA((layers, 11)),
        ],
        compiler_params=pltpu.CompilerParams(vmem_limit_bytes=63 * 2**20),
        name="backward",
    )(lens, block_input, out_grad, gain, bias, qkv_w, out_w, up_w, down_w, *saved)


def body(
    block_input,
    doc_lengths,
    norm_gain,
    norm_bias,
    qkv_weight,
    qkv_bias,
    out_weight,
    out_bias,
    up_weight,
    up_bias,
    down_weight,
    down_bias,
    out_grad,
):
    layers, width = norm_gain.shape
    up_all = lax.all_gather(up_weight, "mlp", axis=2, tiled=True)
    down_all = lax.all_gather(down_weight, "mlp", axis=1, tiled=True)
    up_bias_all = lax.all_gather(up_bias, "mlp", axis=1, tiled=True)
    block_output, *saved = run_forward(
        doc_lengths,
        block_input,
        norm_gain,
        norm_bias,
        qkv_bias,
        out_bias,
        up_bias_all,
        down_bias,
        qkv_weight,
        out_weight,
        up_all,
        down_all,
    )
    input_grad, mlp_grad, att_grad, vec_grad = run_backward(
        doc_lengths,
        block_input,
        out_grad,
        norm_gain,
        norm_bias,
        qkv_weight,
        out_weight,
        up_all,
        down_all,
        saved,
    )
    mlp_grad = lax.psum_scatter(mlp_grad, "mlp", scatter_dimension=1, tiled=False)
    mlp_grad = lax.psum(mlp_grad, "dp").astype(f32)
    att_grad = lax.psum(att_grad, ("dp", "mlp")).astype(f32)
    vec_grad = lax.psum(vec_grad, ("dp", "mlp"))
    return finish(block_output, input_grad, mlp_grad, att_grad, vec_grad)


def finish(block_output, input_grad, mlp_grad, att_grad, vec_grad):
    layers, units, width = mlp_grad.shape
    half = units // 2
    up_grad = jnp.concatenate(
        [mlp_grad[:, at : at + width] for at in range(0, half, width)], axis=2
    )
    down_grad = mlp_grad[:, half:]
    qkv_grad = jnp.concatenate(
        [att_grad[:, at : at + width] for at in range(0, 3 * width, width)], axis=2
    )
    out_w_grad = att_grad[:, 3 * width :]
    out_b_grad = vec_grad[:, 5]
    up_b_all = vec_grad[:, 6 : 6 + units // width].reshape(layers, -1)
    up_b_grad = lax.dynamic_slice_in_dim(up_b_all, lax.axis_index("mlp") * half, half, 1)
    return (
        block_output,
        input_grad,
        vec_grad[:, 0],
        vec_grad[:, 1],
        qkv_grad,
        vec_grad[:, 2:5].reshape(layers, -1),
        out_w_grad,
        out_b_grad,
        up_grad,
        up_b_grad,
        down_grad,
        out_b_grad,
    )


def solution(mesh):
    rows = P(("dp", "mlp"), None)
    return jax.shard_map(
        body,
        mesh=mesh,
        in_specs=(
            rows,
            rows,
            P(),
            P(),
            P(),
            P(),
            P(),
            P(),
            P(None, None, "mlp"),
            P(None, "mlp"),
            P(None, "mlp", None),
            P(),
            rows,
        ),
        out_specs=(
            rows,
            rows,
            P(),
            P(),
            P(),
            P(),
            P(),
            P(),
            P(None, None, "mlp"),
            P(None, "mlp"),
            P(None, "mlp", None),
            P(),
        ),
        check_vma=False,
    )
```

time: 1270 us -> 854 us (0.67)
  matrix products: 369 us -> 0 us
  waiting for transfers between devices: 325 us -> 681 us
  other arithmetic: 274 us -> 5.69 us
  local copies, waits for them, and re-layouts: 196 us -> 21.5 us
  Pallas kernels: 0 us -> 118 us
  blocking collectives: 74.4 us -> 5.32 us
    dot_general x52 -> x0, matrix products: 369 us -> none  [the longest x8 71.1 us: attend_rows(): jnp.einsum('qhd,khd->hqk', query_block, key_rows, preferred_element_type=...]
    unnamed x10 -> x7, waiting for transfers between devices: 0.67 us -> 199 us
    sub x8 -> x0, other arithmetic: 177 us -> none  [attend_rows(): expo = jnp.exp(scores - row_top)]
    pallas_call x0 -> x2, Pallas kernels: none -> 118 us  [the longest x1 72.1 us: run_backward(): pl.pallas_call(backward_kernel, out_shape=(shape((tokens, width), f32), s...]
    psum x2 -> x3, waiting for transfers between devices: 263 us -> 369 us  [the longest x1 144 us: body(): att_grad = lax.psum(att_grad, ('dp', 'mlp')).astype(f32)]
    all_gather x4 -> x2, waiting for transfers between devices: 13 us -> 113 us  [the longest x1 58.3 us: body(): down_all = lax.all_gather(down_weight, 'mlp', axis=1, tiled=True)]
    dynamic_update_slice x8 -> x0, local copies, waits for them, and re-layouts: 86.8 us -> none  [attention_forward(): lax.map(one_block, (queries.reshape(block_count, block_rows, head_count,...]
    psum x2 -> x0, blocking collectives: 74.4 us -> none  [the longest x1 39.7 us: body(): lax.psum((grad_gain, grad_bias, grad_qkv_w, grad_qkv_b, grad_out_w, grad_...]
  transfers between devices with their start and end apart: 10 -> 6, of which waited for: 5 -> 6; matrix products, arithmetic and copies ran while one was open for 59% -> 2% of each run, Pallas kernels for 0% -> 0%
where the time goes in v1:
time: 854 us; the launch traced here: 846 us
  waiting for transfers between devices  681 us (80%)
  Pallas kernels  118 us (14%)
  local copies, waits for them, and re-layouts  21.5 us (3%)
  between operations  14.6 us (2%)
    unnamed x7, waiting for transfers between devices  199 us
    psum x1, waiting for transfers between devices, body(): att_grad = lax.psum(att_grad, ('dp', 'mlp')).astype(f32)  144 us
    psum x1, waiting for transfers between devices, body(): vec_grad = lax.psum(vec_grad, ('dp', 'mlp'))  118 us
    psum x1, waiting for transfers between devices, body(): mlp_grad = lax.psum(mlp_grad, 'dp').astype(f32)  107 us
    pallas_call x1, Pallas kernels, run_backward(): pl.pallas_call(backward_kernel, out_shape=(shape((tokens, width), f32), s...  72.1 us
    all_gather x1, waiting for transfers between devices, body(): down_all = lax.all_gather(down_weight, 'mlp', axis=1, tiled=True)  58.3 us
    all_gather x1, waiting for transfers between devices, body(): up_all = lax.all_gather(up_weight, 'mlp', axis=2, tiled=True)  55 us
    pallas_call x1, Pallas kernels, run_forward(): pl.pallas_call(forward_kernel, out_shape=(shape((tokens, width), bf16), s...  45.8 us
  transfers between devices with their start and end apart: 6, of which 6 were waited for; matrix products, arithmetic and copies ran while one was open for 2% of the time, Pallas kernels for 0%

profile of v1, /device:TPU:0, one launch (start us, length us, event | category | flops | bytes accessed | tf_op | source)
XLA Modules:
  0.0 846.2 jit_solution(17485327544039554266)
XLA Ops:
  7.2 0.7 all-gather.3.cloned.1.call-update
  8.0 0.7 all-gather.5.cloned.1.call-update
  8.7 0.0 all-reduce.12.cloned.1.call-start
  8.7 5.3 all_gather.9.up_bias
  14.1 55.0 %all-gather.3.cloned.1.call-done.up_w_h = bf16[2,512,2048]{2,1,0:T(8,128)(2,1)} async-done(((bf16[2,512,1024]{2,1,0:T(8,128)(2,1)}), bf16[2,512,2048]{2,1,0:T(8,128)(2,1)}) %all-gather.3.cloned.1.call-update) | async-done | bytes 4194320 | tf_op jit(solution)/shard_map/all_gather | solution.py:661
  69.0 58.3 %all-gather.5.cloned.1.call-done.down_w_h = bf16[2,2048,512]{2,1,0:T(8,128)(2,1)} async-done(((bf16[2,1024,512]{2,1,0:T(8,128)(2,1)}), bf16[2,2048,512]{2,1,0:T(8,128)(2,1)}) %all-gather.5.cloned.1.call-update) | async-done | bytes 4194320 | tf_op jit(solution)/shard_map/all_gather | solution.py:662
  127.4 45.8 %forward.1 = (bf16[1024,512]{1,0:T(8,128)(2,1)}, f32[1024,512]{1,0:T(8,128)}, bf16[2,512,1024]{2,1,0:T(8,128)(2,1)}, bf16[2,1536,1024]{2,1,0:T(8,128)(2,1)}, bf1...) custom-call(s32[1,4]{1,0:T(1,128)} %lens.3, ...), custom_call_target="tpu_custom_call" | custom-call | tf_op jit(solution)/shard_map/forward/pallas_call | solution.py:551
  173.1 72.1 %backward.1 = (f32[1024,512]{1,0:T(8,128)}, bf16[2,2,2048,512]{3,2,1,0:T(8,128)(2,1)}, bf16[2,2048,512]{2,1,0:T(8,128)(2,1)}, f32[2,16,512]{2,1,0:T(8,128)}) custom-call(s32[1,4]{1,0:T(1,128)} %lens.3, bf16[1024,512]{1,0:T(8,128)(2,1)} %block_input.3, bf16[1024,512]{1,0:T(8,128)(2,1)} %out_grad.1, bf16[2,512]{1,0:T(2,128)(2,1)} %gain.3, ...), custom_call_target="tpu_custom_call" | custom-call | tf_op jit(solution)/shard_map/backward/pallas_call | solution.py:602
  245.3 0.0 all-reduce.6.cloned.1.call-start
  245.4 0.5 all-reduce.6.cloned.1.call-update
  245.9 0.5 all-reduce.8.cloned.1.call-update
  246.5 0.0 all-reduce.10.cloned.1.call-start
  246.5 0.6 dynamic-slice
  247.1 196.4 %all-reduce.12.cloned.1.call-done = bf16[2,2,2048,512]{3,2,1,0:T(8,128)(2,1)} async-done(((bf16[2,2,2048,512]{3,2,1,0:T(8,128)(2,1)}), bf16[2,2,2048,512]{3,2,1,0:T(8,128)(2,1)}) %all-reduce.12.cloned.1.call-update) | async-done | bytes 8388624
  443.5 5.1 dynamic-slice_bitcast_fusion
  448.6 118.2 %all-reduce.6.cloned.1.call-done = f32[2,16,512]{2,1,0:T(8,128)} async-done(((f32[2,16,512]{2,1,0:T(8,128)}), f32[2,16,512]{2,1,0:T(8,128)}) %all-reduce.6.cloned.1.call-update) | async-done | bytes 65552 | tf_op jit(solution)/shard_map/psum | solution.py:693
  566.8 0.9 fusion.2
  567.7 0.6 copy.35
  568.3 0.8 slice_bitcast_fusion.1
  569.1 0.6 copy.30
  569.7 0.8 slice_bitcast_fusion
  570.5 0.6 copy_bitcast_fusion
  571.1 0.6 constant_dynamic-slice_fusion
  571.7 143.6 %all-reduce.8.cloned.1.call-done = bf16[2,2048,512]{2,1,0:T(8,128)(2,1)} async-done(((bf16[2,2048,512]{2,1,0:T(8,128)(2,1)}), bf16[2,2048,512]{2,1,0:T(8,128)(2,1)}) %all-reduce.8.cloned.1.call-update) | async-done | bytes 4194320 | tf_op jit(solution)/shard_map/psum | solution.py:692
  715.3 4.5 fusion.1
  719.8 3.1 pad_maximum_fusion
  722.9 106.9 %all-reduce.10.cloned.1.call-done = bf16[2,2048,512]{2,1,0:T(8,128)(2,1)} async-done(((bf16[2,2048,512]{2,1,0:T(8,128)(2,1)}), bf16[2,2048,512]{2,1,0:T(8,128)(2,1)}) %all-reduce.10.cloned.1.call-update) | async-done | bytes 4194320 | tf_op jit(solution)/shard_map/psum | solution.py:691
  829.9 2.1 fusion
  832.0 2.5 pad_maximum_fusion.1
  834.5 1.2 copy-done
  835.7 2.6 slice.59
  838.3 0.6 copy.41
  (13 shorter events, 0.2 us)
Async XLA Ops:
  7.2 1.5 copy-start.2
  7.2 61.9 %all-gather.3.cloned.1.call-start = ((), (), s32[]{:S(2)}) async-start(), calls=%async_computation | async-start | bytes 6291456 | tf_op jit(solution)/shard_map/all_gather | solution.py:661
  7.9 119.4 %all-gather.5.cloned.1.call-start = ((), (), s32[]{:S(2)}) async-start(), calls=%async_computation.1 | async-start | bytes 6291456 | tf_op jit(solution)/shard_map/all_gather | solution.py:662
  8.7 434.8 %all-reduce.12.cloned.1.call-start = ((), (), s32[]{:S(2)}) async-start(), calls=%async_computation.5 | async-start | bytes 16777216
  245.3 1.2 copy-start.3
  245.3 321.5 %all-reduce.6.cloned.1.call-start = ((), (), s32[]{:S(2)}) async-start(), calls=%async_computation.2 | async-start | bytes 131072 | tf_op jit(solution)/shard_map/psum | solution.py:693
  245.9 469.4 %all-reduce.8.cloned.1.call-start = ((), (), s32[]{:S(2)}) async-start(), calls=%async_computation.3 | async-start | bytes 8388608 | tf_op jit(solution)/shard_map/psum | solution.py:692
  246.5 583.4 %all-reduce.10.cloned.1.call-start = ((), (), s32[]{:S(2)}) async-start(), calls=%async_computation.4 | async-start | bytes 8388608 | tf_op jit(solution)/shard_map/psum | solution.py:691
  571.1 267.2 %copy-start.1 = (f32[2,512]{1,0:T(2,128)}, f32[2,512]{1,0:T(2,128)S(1)}, u32[]{:S(2)}) copy-start(f32[2,512]{1,0:T(2,128)S(1)} %get-tuple-element.70) | copy-start | bytes 12292
  832.0 3.7 copy-start
Sparse Core Ops, SparseCore 0:
  9.6 59.4 all-gather.2
  70.6 56.7 all-gather.4
  245.4 198.0 all-reduce.11
  448.9 117.8 all-reduce.5
  572.8 142.5 all-reduce.7
  719.4 110.3 all-reduce.9
